TPU v7x, 32 devices: a whole 2x2x4 slice. The times are simulated.
32 devices in a mesh: dp: 16 (over z, y, x), space: 2 (over core).
Axes of the slice: x: 2, y: 2, z: 4, core: 2. Of those that a mesh axis runs over, the one named last changes fastest.
Arguments:
- image: bfloat16 [16, 8, 8, 8, 128], P('dp', 'space'), may hold values from -30 to 30
- cotangent: bfloat16 [16, 8, 8, 8, 128], P('dp', 'space'), may hold values from -30 to 30
- first_weight: bfloat16 [3456, 128], P('dp'), may hold values from -0.109375 to 0.109375
- second_weight: bfloat16 [3456, 128], P('dp'), may hold values from -0.109375 to 0.109375
Outputs:
- output: bfloat16 [16, 8, 8, 8, 128], P('dp', 'space')
- image_grad: bfloat16 [16, 8, 8, 8, 128], P('dp', 'space')
- first_grad: float32 [3456, 128], P('dp')
- second_grad: float32 [3456, 128], P('dp')
All inputs are finite; a program needn't handle non-finite values.
Results may differ from a plain program's by a relative error of at most 0.013.
Values may be sent and summed in bfloat16 or wider, within the bound.
A program may use at most 64 MiB of HBM per device.

v0:
```python
import math

import jax
import jax.numpy as jnp
from jax import lax
from jax.sharding import PartitionSpec as P

EPSILON = 1e-05


def with_halo(cells, sides, width):
    for axis, dim in sides:
        count = lax.axis_size(axis)
        ends = count - 1
        head = lax.slice_in_dim(cells, 0, width, axis=dim)
        tail = lax.slice_in_dim(cells, cells.shape[dim] - width, cells.shape[dim], axis=dim)
        cells = jnp.concatenate(
            [
                lax.ppermute(tail, axis, [(i, (i + 1) % count) for i in range(ends)]),
                cells,
                lax.ppermute(head, axis, [((i + 1) % count, i) for i in range(ends)]),
            ],
            axis=dim,
        )
    return cells


def gelu_value(values):
    return 0.5 * values * (1.0 + lax.erf(values * 0.7071067811865476))


def gelu_slope(values):
    return (
        0.5 * (1.0 + lax.erf(values * 0.7071067811865476))
        + values * jnp.exp(-0.5 * values * values) * 0.3989422804014327
    )


def columns(deep):
    depth = deep.shape[0] - 2
    height, width, channels = (deep.shape[1], deep.shape[2], deep.shape[3])
    padded = jnp.pad(deep, ((0, 0), (1, 1), (1, 1), (0, 0)))
    pieces = [
        padded[first : first + depth, second : second + height, third : third + width, :]
        for first in range(3)
        for second in range(3)
        for third in range(3)
    ]
    return jnp.concatenate(pieces, axis=-1).reshape(depth * height * width, 27 * channels)


def reverse_taps(weight):
    channels = weight.shape[1]
    return (
        weight.reshape(27, channels, channels)[::-1]
        .transpose(0, 2, 1)
        .reshape(27 * channels, channels)
    )


def local(image, cotangent, first_weight, second_weight):
    slab = image[0]
    depth, height, width, channels = slab.shape
    cells = depth * height * width
    patch_cells = cells * lax.axis_size("space")
    factor = 1.0 / math.sqrt(patch_cells * lax.axis_size("dp"))

    def unfold_slab(volume):
        deep = with_halo(volume, (("space", 0),), 1)
        return columns(deep)

    def normalize(values):
        totals, squares = lax.psum(
            (jnp.sum(values, axis=0), jnp.sum(values * values, axis=0)), "space"
        )
        average = totals / patch_cells
        inverse = lax.rsqrt(squares / patch_cells - average * average + EPSILON)
        return ((values - average) * inverse, inverse)

    def norm_back(grad, normed, inverse):
        plain_total, paired_total = lax.psum(
            (jnp.sum(grad, axis=0), jnp.sum(grad * normed, axis=0)), "space"
        )
        return inverse * (grad - plain_total / patch_cells - normed * (paired_total / patch_cells))

    def apply_weight(unfolded, shard):
        whole = lax.all_gather(shard, "dp", axis=0, tiled=True)
        return (jnp.dot(unfolded, whole, preferred_element_type=jnp.float32), shard)

    def weight_again(kept):
        whole = lax.all_gather(kept, "dp", axis=0, tiled=True)
        return reverse_taps(whole)

    def reduce_grad(unfolded, delta):
        own_rows = lax.psum_scatter(
            lax.dot_general(
                unfolded, delta, (((0,), (0,)), ((), ())), preferred_element_type=jnp.float32
            ),
            "dp",
            scatter_dimension=0,
            tiled=True,
        )
        return lax.psum(own_rows, "space")

    first_columns = unfold_slab(slab)
    first_conv, first_kept = apply_weight(first_columns, first_weight)
    first_norm, first_inverse = normalize(first_conv)
    hidden = gelu_value(first_norm).astype(jnp.bfloat16)
    second_columns = unfold_slab(hidden.reshape(depth, height, width, channels))
    second_conv, second_kept = apply_weight(second_columns, second_weight)
    second_norm, second_inverse = normalize(second_conv)
    summed = slab.reshape(cells, channels).astype(jnp.float32) + second_norm
    output = gelu_value(summed).astype(jnp.bfloat16)
    outer_grad = cotangent[0].reshape(cells, channels).astype(jnp.float32) * gelu_slope(summed)
    second_delta = norm_back(outer_grad, second_norm, second_inverse).astype(jnp.bfloat16)
    second_grad = reduce_grad(second_columns, second_delta)
    inner_grad = jnp.dot(
        unfold_slab(second_delta.reshape(depth, height, width, channels)),
        weight_again(second_kept),
        preferred_element_type=jnp.float32,
    )
    first_delta = norm_back(inner_grad * gelu_slope(first_norm), first_norm, first_inverse).astype(
        jnp.bfloat16
    )
    first_grad = reduce_grad(first_columns, first_delta)
    backward_term = jnp.dot(
        unfold_slab(first_delta.reshape(depth, height, width, channels)),
        weight_again(first_kept),
        preferred_element_type=jnp.float32,
    )
    image_grad = (outer_grad + backward_term).astype(jnp.bfloat16)
    return (
        output.reshape(image.shape),
        image_grad.reshape(image.shape),
        first_grad * factor,
        second_grad * factor,
    )


def solution(mesh):
    return jax.shard_map(
        local,
        mesh=mesh,
        in_specs=(
            P("dp", "space", None, None, None),
            P("dp", "space", None, None, None),
            P("dp", None),
            P("dp", None),
        ),
        out_specs=(
            P("dp", "space", None, None, None),
            P("dp", "space", None, None, None),
            P("dp", None),
            P("dp", None),
        ),
        check_vma=False,
    )
```

profile of v0, /device:TPU:0, one launch (start us, length us, event | category | flops | bytes accessed | tf_op | source)
XLA Modules:
  0.0 422.5 jit_solution(17913436711791896058)
XLA Ops:
  8.0 2.3 collective-permute-start
  10.3 1.4 collective-permute-start.1
  11.7 47.7 %all_gather.8 = bf16[3456,128]{1,0:T(8,128)(2,1)S(1)} all-gather(bf16[216,128]{1,0:T(8,128)(2,1)} %param.6), channel_id=1, replica_groups=mesh['dp'=16,'space'=2] {'dp'}, dimensions={0}, use_global_device_ids=true | all-gather | bytes 940032 | tf_op jit(solution)/shard_map/all_gather | solution.py:87
  59.5 41.3 %all_gather.9 = bf16[3456,128]{1,0:T(8,128)(2,1)S(1)} all-gather(bf16[216,128]{1,0:T(8,128)(2,1)} %param.7), channel_id=1, replica_groups=mesh['dp'=16,'space'=2] {'dp'}, dimensions={0}, use_global_device_ids=true | all-gather | bytes 940032 | tf_op jit(solution)/shard_map/all_gather | solution.py:87
  100.8 1.0 reverse_bitcast_fusion.1
  102.9 1.3 fusion.24
  104.1 2.4 all-reduce.9
  106.6 0.9 multiply_convert_fusion.3
  108.8 2.1 collective-permute-start.2
  110.9 1.3 collective-permute-start.3
  112.2 1.1 reverse_bitcast_fusion
  113.2 2.2 copy.10
  115.4 1.9 copy.11
  117.4 0.9 select_maximum_fusion.4
  120.5 1.3 fusion.23
  121.8 3.8 all-reduce.8
  125.7 1.7 fusion.22
  127.3 2.5 all-reduce.7
  129.8 0.9 multiply_convert_fusion.1
  130.8 2.2 collective-permute-start.4
  133.0 1.3 collective-permute-start.5
  134.3 3.4 fusion.35
  140.1 3.2 all-reduce.6
  143.4 2.2 collective-permute-start.6
  145.7 1.3 collective-permute-start.7
  147.0 1.9 fusion.34
  166.8 96.1 %reduce-scatter.9.cloned.1.call-done = f32[216,128]{1,0:T(8,128)} async-done(((f32[3456,128]{1,0:T(8,128)}), f32[216,128]{1,0:T(8,128)}) %reduce-scatter.9.cloned.1.call-update) | async-done | bytes 110608
  262.9 130.4 %reduce-scatter.7.cloned.1.call-done = f32[216,128]{1,0:T(8,128)} async-done(((f32[3456,128]{1,0:T(8,128)}), f32[216,128]{1,0:T(8,128)}) %reduce-scatter.7.cloned.1.call-update) | async-done | bytes 110608
  393.4 2.7 fusion
  396.1 16.8 %all-reduce.13.cloned.1.call-done = (f32[216,128]{1,0:T(8,128)}, f32[216,128]{1,0:T(8,128)}) async-done(((f32[216,128]{1,0:T(8,128)}, f32[216,128]{1,0:T(8,128)}), (f32[216,128]{1,0:T(8,128)}, f32[216,128]{1,0:T(8,128)})) %all-reduce.13.cloned.1.call-update) | async-done | bytes 221200 | tf_op jit(solution)/shard_map/psum | solution.py:103
  412.9 1.6 broadcast_multiply_fusion.1
  414.5 1.6 broadcast_multiply_fusion
  (174 shorter events, 25.0 us)
Async XLA Ops:
  7.2 255.8 %reduce-scatter.9.cloned.1.call-start = ((), (), s32[]{:S(2)}) async-start(), calls=%async_computation.3 | async-start | bytes 1880064
  8.0 93.8 %collective-permute-start = (bf16[1,8,8,128]{3,2,1,0:T(8,128)(2,1)S(1)}, bf16[1,8,8,128]{3,2,1,0:T(8,128)(2,1)S(1)}, u32[]{:S(2)}, u32[]{:S(2)}) collective-permute-start(bf16[1,8,8,128]{3,2,1,0:T(8,128)(2,1)S(1)} %get-tuple-element.134), channel_id=1, source_target_pairs={{0,1},{2,3},{4,5},{6,7},{8,9},{10,11},{12,13},{14,15},{16,17},{18,... | collective-permute-start | bytes 49160 | tf_op jit(solution)/shard_map/ppermute | solution.py:19
  10.3 91.5 %copy-start.3 = (bf16[1,4,8,8,128]{4,3,2,1,0:T(8,128)(2,1)S(1)}, bf16[1,4,8,8,128]{4,3,2,1,0:T(8,128)(2,1)}, u32[]{:S(2)}) copy-start(bf16[1,4,8,8,128]{4,3,2,1,0:T(8,128)(2,1)} %param.4) | copy-start | bytes 196612
  10.3 91.4 %collective-permute-start.1 = (bf16[1,8,8,128]{3,2,1,0:T(8,128)(2,1)S(1)}, bf16[1,8,8,128]{3,2,1,0:T(8,128)(2,1)S(1)}, u32[]{:S(2)}, u32[]{:S(2)}) collective-permute-start(bf16[1,8,8,128]{3,2,1,0:T(8,128)(2,1)S(1)} %get-tuple-element.135), channel_id=1, source_target_pairs={{1,0},{3,2},{5,4},{7,6},{9,8},{11,10},{13,12},{15,14},{17,16},{19,... | collective-permute-start | bytes 49160 | tf_op jit(solution)/shard_map/ppermute | solution.py:21
  106.6 2.2 copy-start.7
  106.6 2.2 copy-start.10
  107.6 0.6 copy-start.5
  108.8 8.5 %collective-permute-start.2 = (bf16[1,8,8,128]{3,2,1,0:T(8,128)(2,1)}, bf16[1,8,8,128]{3,2,1,0:T(8,128)(2,1)S(1)}, u32[]{:S(2)}, u32[]{:S(2)}) collective-permute-start(bf16[1,8,8,128]{3,2,1,0:T(8,128)(2,1)} %get-tuple-element.130), channel_id=1, source_target_pairs={{0,1},{2,3},{4,5},{6,7},{8,9},{10,11},{12,13},{14,15},{16,17},{18,... | collective-permute-start | bytes 49160 | tf_op jit(solution)/shard_map/ppermute | solution.py:19
  110.9 6.5 %collective-permute-start.3 = (bf16[1,8,8,128]{3,2,1,0:T(8,128)(2,1)}, bf16[1,8,8,128]{3,2,1,0:T(8,128)(2,1)}, u32[]{:S(2)}, u32[]{:S(2)}) collective-permute-start(bf16[1,8,8,128]{3,2,1,0:T(8,128)(2,1)} %get-tuple-element.131), channel_id=1, source_target_pairs={{1,0},{3,2},{5,4},{7,6},{9,8},{11,10},{13,12},{15,14},{17,16},{19,... | collective-permute-start | bytes 49160 | tf_op jit(solution)/shard_map/ppermute | solution.py:21
  118.3 0.8 copy-start.6
  118.4 1.7 copy-start.1
  118.4 1.7 copy-start.8
  118.4 1.7 copy-start.11
  120.5 1.3 copy-start
  130.8 7.0 %collective-permute-start.4 = (bf16[1,8,8,128]{3,2,1,0:T(8,128)(2,1)S(1)}, bf16[1,8,8,128]{3,2,1,0:T(8,128)(2,1)S(1)}, u32[]{:S(2)}, u32[]{:S(2)}) collective-permute-start(bf16[1,8,8,128]{3,2,1,0:T(8,128)(2,1)S(1)} %get-tuple-element.126), channel_id=1, source_target_pairs={{0,1},{2,3},{4,5},{6,7},{8,9},{10,11},{12,13},{14,15},{16,17},{18,... | collective-permute-start | bytes 49160 | tf_op jit(solution)/shard_map/ppermute | solution.py:19
  133.0 4.8 %collective-permute-start.5 = (bf16[1,8,8,128]{3,2,1,0:T(8,128)(2,1)S(1)}, bf16[1,8,8,128]{3,2,1,0:T(8,128)(2,1)S(1)}, u32[]{:S(2)}, u32[]{:S(2)}) collective-permute-start(bf16[1,8,8,128]{3,2,1,0:T(8,128)(2,1)S(1)} %get-tuple-element.127), channel_id=1, source_target_pairs={{1,0},{3,2},{5,4},{7,6},{9,8},{11,10},{13,12},{15,14},{17,16},{19,... | collective-permute-start | bytes 49160 | tf_op jit(solution)/shard_map/ppermute | solution.py:21
  137.7 255.6 %reduce-scatter.7.cloned.1.call-start = ((), (), s32[]{:S(2)}) async-start(), calls=%async_computation.2 | async-start | bytes 1880064
  138.2 0.9 copy-start.2
  138.2 1.2 copy-start.4
  138.3 1.2 copy-start.9
  138.3 1.2 copy-start.12
  143.4 5.5 %collective-permute-start.6 = (bf16[1,8,8,128]{3,2,1,0:T(8,128)(2,1)S(1)}, bf16[1,8,8,128]{3,2,1,0:T(8,128)(2,1)S(1)}, u32[]{:S(2)}, u32[]{:S(2)}) collective-permute-start(bf16[1,8,8,128]{3,2,1,0:T(8,128)(2,1)S(1)} %get-tuple-element.122), channel_id=1, source_target_pairs={{0,1},{2,3},{4,5},{6,7},{8,9},{10,11},{12,13},{14,15},{16,17},{18,... | collective-permute-start | bytes 49160 | tf_op jit(solution)/shard_map/ppermute | solution.py:19
  145.7 3.3 collective-permute-start.7
  148.9 264.0 %all-reduce.13.cloned.1.call-start = ((), (), s32[]{:S(2)}) async-start(), calls=%async_computation.4 | async-start | bytes 442368 | tf_op jit(solution)/shard_map/psum | solution.py:103
Sparse Core Ops, SparseCore 0:
  137.9 125.0 reduce-scatter.8
  267.8 125.5 reduce-scatter.6
  395.7 17.1 all-reduce.12
where the time goes:
time: 423 us
  waiting for transfers between devices  243 us (57%)
  blocking collectives  101 us (24%)
  local copies, waits for them, and re-layouts  29.2 us (7%)
  between operations  14.7 us (3%)
  starting transfers between devices  14.3 us (3%)
  matrix products  11.2 us (3%)
  other arithmetic  8.8 us (2%)
    unnamed x5, waiting for transfers between devices  227 us
    all_gather x2, blocking collectives, apply_weight(): whole = lax.all_gather(shard, 'dp', axis=0, tiled=True)  89 us
    unnamed x129, local copies, waits for them, and re-layouts  19.9 us
    psum x1, waiting for transfers between devices, reduce_grad(): return lax.psum(own_rows, 'space')  16.8 us
    ppermute x4, starting transfers between devices, with_halo(): lax.ppermute(tail, axis, [(i, (i + 1) % count) for i in range(ends)])  8.9 us
  transfers between devices with their start and end apart: 11, of which 3 were waited for; matrix products, arithmetic and copies ran while one was open for 8% of the time, Pallas kernels for 0%

commit v1 on v0

--- a/solution.py
+++ b/solution.py
@@ -1,9 +1,14 @@
+import functools
 import math
 
 import jax
 import jax.numpy as jnp
 from jax import lax
+from jax.experimental import pallas as pl
+from jax.experimental.pallas import tpu as pltpu
 from jax.sharding import PartitionSpec as P
+
+MESH = pl.DeviceIdType.MESH
 
 EPSILON = 1e-05
 
@@ -137,9 +142,439 @@
     )
 
 
+def group_size(count):
+    size = 1
+    while size * size < count and count % (2 * size) == 0:
+        size *= 2
+    return size
+
+
+def remote(src, dst, send_sem, recv_sem, device):
+    return pltpu.make_async_remote_copy(
+        src_ref=src,
+        dst_ref=dst,
+        send_sem=send_sem,
+        recv_sem=recv_sem,
+        device_id=device,
+        device_id_type=MESH,
+    )
+
+
+def block_kernel(
+    sizes,
+    image_ref,
+    cotangent_ref,
+    first_ref,
+    second_ref,
+    output_ref,
+    image_grad_ref,
+    first_grad_ref,
+    second_grad_ref,
+    fields,
+    gathered,
+    rows_f32,
+    weights,
+    turned,
+    image_cols,
+    hidden_cols,
+    delta_cols,
+    planes,
+    grad_rows,
+    grad_send,
+    grad_recv,
+    line_send,
+    line_recv,
+    halves,
+    summed_ref,
+    outer_ref,
+    field_send,
+    field_recv,
+    line_ws,
+    line_wr,
+    plane_ws,
+    plane_wr,
+    core_ws,
+    core_wr,
+    plane_gs,
+    plane_gr,
+    line_gs,
+    line_gr,
+    core_gs,
+    core_gr,
+):
+    count, inner, depth, height, width, channels, rows = sizes
+    outer = count // inner
+    half = gathered.shape[3]
+    cells = depth * height * width
+    own_cells = cells // 2
+    area = height * width
+    factor = 1.0 / math.sqrt(cells * count)
+    me = lax.axis_index("dp")
+    core = lax.axis_index("space")
+    z = lax.div(me, inner)
+    p = lax.rem(me, inner)
+    sibling = (me, 1 - core)
+
+    def line_peer(s):
+        return lax.rem(z + s, outer), lax.rem(z - s + outer, outer)
+
+    def plane_peer(s):
+        return lax.rem(p + s, inner), lax.rem(p - s + inner, inner)
+
+    for w, ref in enumerate((first_ref, second_ref)):
+        own = jnp.concatenate(
+            [
+                ref[...].astype(jnp.float32),
+                jnp.zeros((2 * half - rows, channels), jnp.float32),
+            ],
+            axis=0,
+        )
+        mine = jnp.where(core == 0, own[:half], own[half:])
+        gathered[w, core, me] = mine.astype(jnp.bfloat16)
+
+    barrier = pltpu.get_barrier_semaphore()
+    partners = [sibling]
+    partners += [(line_peer(s)[0] * inner + p, core) for s in range(1, outer)]
+    partners += [(z * inner + plane_peer(s)[0], core) for s in range(1, inner)]
+    for device in partners:
+        pl.semaphore_signal(barrier, inc=1, device_id=device, device_id_type=MESH)
+    pl.semaphore_wait(barrier, len(partners))
+
+    sends = []
+
+    def start(copy):
+        copy.start()
+        sends.append(copy)
+
+    def line_copy(w, s, source, target):
+        place = gathered.at[w, core, source]
+        return remote(place, place, line_ws.at[w, s], line_wr.at[w, s], (target, core))
+
+    def plane_copy(w, t, s, source, target):
+        place = gathered.at[w, core, source]
+        return remote(place, place, plane_ws.at[w, t, s], plane_wr.at[w, t, s], (target, core))
+
+    def core_copy(w, t, which):
+        group = pl.ds(line_peer(t)[1] * inner, inner)
+        place = gathered.at[w, which, group]
+        return remote(place, place, core_ws.at[w, t], core_wr.at[w, t], sibling)
+
+    def send_line(w):
+        for s in range(1, outer):
+            start(line_copy(w, s, me, line_peer(s)[0] * inner + p))
+
+    def send_plane(w):
+        for t in range(outer):
+            source = line_peer(t)[1] * inner + p
+            if t > 0:
+                line_copy(w, t, source, me).wait_recv()
+            for s in range(1, inner):
+                start(plane_copy(w, t, s, source, z * inner + plane_peer(s)[0]))
+
+    def send_core(w):
+        for t in range(outer):
+            for s in range(1, inner):
+                source = line_peer(t)[1] * inner + plane_peer(s)[1]
+                plane_copy(w, t, s, source, me).wait_recv()
+            start(core_copy(w, t, core))
+
+    def finish_weight(w):
+        for t in range(outer):
+            core_copy(w, t, 1 - core).wait_recv()
+        for d in range(count):
+            base = d * rows
+            rows_f32[base : base + half, :] = gathered[w, 0, d].astype(jnp.float32)
+            rows_f32[base + half : base + rows, :] = gathered[w, 1, d].astype(jnp.float32)[
+                : rows - half
+            ]
+        for k in range(27):
+            block = rows_f32[k * channels : (k + 1) * channels, :].astype(jnp.bfloat16)
+            a, rest = divmod(k, 9)
+            weights[w, rest * channels : (rest + 1) * channels, a * channels : (a + 1) * channels] = block
+            a, rest = divmod(26 - k, 9)
+            turned[w, a * channels : (a + 1) * channels, rest * channels : (rest + 1) * channels] = block
+
+    def spread(cols, values):
+        field = values.reshape(depth * height, width, channels)
+        place = lax.broadcasted_iota(jnp.int32, field.shape, 1)
+        left = jnp.where(place == 0, 0.0, pltpu.roll(field, 1, 1))
+        right = jnp.where(place == width - 1, 0.0, pltpu.roll(field, width - 1, 1))
+        for c, moved in enumerate((left, field, right)):
+            moved = moved.reshape(depth, height, width, channels)
+            edge = jnp.zeros((depth, 1, width, channels), jnp.float32)
+            for b in range(3):
+                if b == 0:
+                    piece = jnp.concatenate([edge, moved[:, :-1]], axis=1)
+                elif b == 1:
+                    piece = moved
+                else:
+                    piece = jnp.concatenate([moved[:, 1:], edge], axis=1)
+                k = 3 * b + c
+                cols[:, k * channels : (k + 1) * channels] = piece.reshape(cells, channels).astype(
+                    jnp.bfloat16
+                )
+
+    edge_plane = jnp.zeros((area, channels), jnp.float32)
+
+    def fold_planes(parts):
+        before, here, after = (parts[:, a * channels : (a + 1) * channels] for a in range(3))
+        return (
+            jnp.concatenate([edge_plane, before[:-area]], axis=0)
+            + here
+            + jnp.concatenate([after[area:], edge_plane], axis=0)
+        )
+
+    def forward(cols, w):
+        return fold_planes(jnp.dot(cols[...], weights[w], preferred_element_type=jnp.float32))
+
+    def backward(cols, w):
+        return fold_planes(
+            lax.dot_general(
+                cols[...],
+                turned[w],
+                (((1,), (1,)), ((), ())),
+                preferred_element_type=jnp.float32,
+            )
+        )
+
+    def normalize(values):
+        average = jnp.sum(values, axis=0, keepdims=True) / cells
+        square_mean = jnp.sum(values * values, axis=0, keepdims=True) / cells
+        inverse = lax.rsqrt(square_mean - average * average + EPSILON)
+        return (values - average) * inverse, inverse
+
+    def norm_back(grad, normed, inverse):
+        plain = jnp.sum(grad, axis=0, keepdims=True) / cells
+        paired = jnp.sum(grad * normed, axis=0, keepdims=True) / cells
+        return inverse * (grad - plain - normed * paired)
+
+    def weight_grad(cols, delta, g):
+        planes[:, :channels] = jnp.concatenate([delta[area:], edge_plane], axis=0).astype(
+            jnp.bfloat16
+        )
+        planes[:, channels : 2 * channels] = delta.astype(jnp.bfloat16)
+        planes[:, 2 * channels :] = jnp.concatenate([edge_plane, delta[:-area]], axis=0).astype(
+            jnp.bfloat16
+        )
+        result = lax.dot_general(
+            cols[...], planes[...], (((0,), (0,)), ((), ())), preferred_element_type=jnp.float32
+        )
+        for a in range(3):
+            for rest in range(9):
+                k = 9 * a + rest
+                grad_rows[g, k * channels : (k + 1) * channels, :] = result[
+                    rest * channels : (rest + 1) * channels, a * channels : (a + 1) * channels
+                ]
+        for s in range(1, inner):
+            target = plane_peer(s)[0]
+            for t in range(outer):
+                grad_send[g, s, t] = own_part(g, t * inner + target).astype(jnp.bfloat16)
+            start(plane_grad_copy(g, s, z * inner + target))
+
+    def own_part(g, d):
+        offset = pl.multiple_of(d * rows + core * half, 8)
+        return grad_rows[g, pl.ds(offset, half), :]
+
+    def plane_grad_copy(g, s, target):
+        return remote(
+            grad_send.at[g, s],
+            grad_recv.at[g, s],
+            plane_gs.at[g, s],
+            plane_gr.at[g, s],
+            (target, core),
+        )
+
+    def line_grad_copy(g, t, target):
+        return remote(
+            line_send.at[g, t],
+            line_recv.at[g, t],
+            line_gs.at[g, t],
+            line_gr.at[g, t],
+            (target, core),
+        )
+
+    def core_grad_copy(g, which):
+        place = halves.at[g, which]
+        return remote(place, place, core_gs.at[g], core_gr.at[g], sibling)
+
+    def reduce_plane(g):
+        for s in range(1, inner):
+            plane_grad_copy(g, s, me).wait_recv()
+        for t in range(1, outer):
+            target = line_peer(t)[0]
+            total = own_part(g, target * inner + p)
+            for s in range(1, inner):
+                total = total + grad_recv[g, s, target].astype(jnp.float32)
+            line_send[g, t] = total.astype(jnp.bfloat16)
+            start(line_grad_copy(g, t, target * inner + p))
+        total = own_part(g, me)
+        for s in range(1, inner):
+            total = total + grad_recv[g, s, z].astype(jnp.float32)
+        halves[g, core] = total
+
+    def reduce_line(g):
+        total = halves[g, core]
+        for t in range(1, outer):
+            line_grad_copy(g, t, me).wait_recv()
+            total = total + line_recv[g, t].astype(jnp.float32)
+        halves[g, core] = total * factor
+        start(core_grad_copy(g, core))
+
+    def write_grad(g, ref):
+        core_grad_copy(g, 1 - core).wait_recv()
+        ref[0:half, :] = halves[g, 0]
+        ref[half:rows, :] = halves[g, 1][: rows - half]
+
+    send_line(0)
+    own_rows = pl.ds(pl.multiple_of(core * own_cells, own_cells), own_cells)
+    other_rows = pl.ds(pl.multiple_of((1 - core) * own_cells, own_cells), own_cells)
+    for f, ref in enumerate((image_ref, cotangent_ref)):
+        start(
+            remote(ref, fields.at[f, own_rows], field_send.at[f], field_recv.at[f], sibling)
+        )
+        fields[f, own_rows, :] = ref[...]
+    send_line(1)
+    grad_rows[:, count * rows :, :] = jnp.zeros_like(grad_rows[:, count * rows :, :])
+    send_plane(0)
+    for f, ref in enumerate((image_ref, cotangent_ref)):
+        remote(
+            ref, fields.at[f, other_rows], field_send.at[f], field_recv.at[f], sibling
+        ).wait_recv()
+    spread(image_cols, fields[0].astype(jnp.float32))
+    send_core(0)
+    send_plane(1)
+    finish_weight(0)
+
+    first_norm, first_inverse = normalize(forward(image_cols, 0))
+    hidden = gelu_value(first_norm).astype(jnp.bfloat16)
+    spread(hidden_cols, hidden.astype(jnp.float32))
+    send_core(1)
+    finish_weight(1)
+    second_norm, second_inverse = normalize(forward(hidden_cols, 1))
+    summed = fields[0].astype(jnp.float32) + second_norm
+    summed_ref[...] = summed
+    outer_grad = fields[1].astype(jnp.float32) * gelu_slope(summed)
+    outer_ref[...] = outer_grad
+    second_delta = norm_back(outer_grad, second_norm, second_inverse)
+    second_delta = second_delta.astype(jnp.bfloat16).astype(jnp.float32)
+    weight_grad(hidden_cols, second_delta, 1)
+    spread(delta_cols, second_delta)
+    inner_grad = backward(delta_cols, 1)
+    first_delta = norm_back(inner_grad * gelu_slope(first_norm), first_norm, first_inverse)
+    first_delta = first_delta.astype(jnp.bfloat16).astype(jnp.float32)
+    weight_grad(image_cols, first_delta, 0)
+    reduce_plane(1)
+    spread(delta_cols, first_delta)
+    outer_ref[...] = outer_ref[...] + backward(delta_cols, 0)
+    image_grad_ref[...] = outer_ref[own_rows, :].astype(jnp.bfloat16)
+    output_ref[...] = gelu_value(summed_ref[own_rows, :]).astype(jnp.bfloat16)
+    reduce_line(1)
+    reduce_plane(0)
+    write_grad(1, second_grad_ref)
+    reduce_line(0)
+    write_grad(0, first_grad_ref)
+    for copy in sends:
+        copy.wait_send()
+
+
+def fused(count, image, cotangent, first_weight, second_weight):
+    _, depth, height, width, channels = image.shape
+    own_cells = depth * height * width
+    cells = 2 * own_cells
+    rows = first_weight.shape[0]
+    half = -(-rows // 32) * 16
+    inner = group_size(count)
+    outer = count // inner
+    sizes = (count, inner, 2 * depth, height, width, channels, rows)
+    bf16, f32 = jnp.bfloat16, jnp.float32
+    dma = pltpu.SemaphoreType.DMA
+    whole = pl.BlockSpec(memory_space=pltpu.VMEM)
+    output, image_grad, first_grad, second_grad = pl.pallas_call(
+        functools.partial(block_kernel, sizes),
+        out_shape=(
+            jax.ShapeDtypeStruct((own_cells, channels), bf16),
+            jax.ShapeDtypeStruct((own_cells, channels), bf16),
+            jax.ShapeDtypeStruct((rows, channels), f32),
+            jax.ShapeDtypeStruct((rows, channels), f32),
+        ),
+        in_specs=[whole] * 4,
+        out_specs=(whole,) * 4,
+        scratch_shapes=[
+            pltpu.VMEM((2, cells, channels), bf16),
+            pltpu.VMEM((2, 2, count, half, channels), bf16),
+            pltpu.VMEM((27 * channels, channels), f32),
+            pltpu.VMEM((2, 9 * channels, 3 * channels), bf16),
+            pltpu.VMEM((2, 3 * channels, 9 * channels), bf16),
+            pltpu.VMEM((cells, 9 * channels), bf16),
+            pltpu.VMEM((cells, 9 * channels), bf16),
+            pltpu.VMEM((cells, 9 * channels), bf16),
+            pltpu.VMEM((cells, 3 * channels), bf16),
+            pltpu.VMEM((2, 27 * channels + 2 * half - rows, channels), f32),
+            pltpu.VMEM((2, inner, outer, half, channels), bf16),
+            pltpu.VMEM((2, inner, outer, half, channels), bf16),
+            pltpu.VMEM((2, outer, half, channels), bf16),
+            pltpu.VMEM((2, outer, half, channels), bf16),
+            pltpu.VMEM((2, 2, half, channels), f32),
+            pltpu.VMEM((cells, channels), f32),
+            pltpu.VMEM((cells, channels), f32),
+            dma((2,)),
+            dma((2,)),
+            dma((2, outer)),
+            dma((2, outer)),
+            dma((2, outer, inner)),
+            dma((2, outer, inner)),
+            dma((2, outer)),
+            dma((2, outer)),
+            dma((2, inner)),
+            dma((2, inner)),
+            dma((2, outer)),
+            dma((2, outer)),
+            dma((2,)),
+            dma((2,)),
+        ],
+        compiler_params=pltpu.CompilerParams(
+            collective_id=0, has_side_effects=True, vmem_limit_bytes=56 * 1024 * 1024
+        ),
+        cost_estimate=pl.CostEstimate(
+            flops=12 * cells * 27 * channels * channels,
+            bytes_accessed=12 * own_cells * channels,
+            transcendentals=6 * cells * channels,
+        ),
+    )(
+        image.reshape(own_cells, channels),
+        cotangent.reshape(own_cells, channels),
+        first_weight,
+        second_weight,
+    )
+    return output.reshape(image.shape), image_grad.reshape(image.shape), first_grad, second_grad
+
+
+def fits_kernel(count, slabs, image, first_weight):
+    _, depth, height, width, channels = image.shape
+    rows = first_weight.shape[0]
+    inner = group_size(count)
+    return (
+        slabs == 2
+        and image.shape[0] == 1
+        and inner > 1
+        and count // inner > 1
+        and width % 8 == 0
+        and channels % 128 == 0
+        and rows % 8 == 0
+        and depth * height * width <= 512
+    )
+
+
+def block(image, cotangent, first_weight, second_weight):
+    count, slabs = lax.axis_size("dp"), lax.axis_size("space")
+    if fits_kernel(count, slabs, image, first_weight):
+        return fused(count, image, cotangent, first_weight, second_weight)
+    return local(image, cotangent, first_weight, second_weight)
+
+
 def solution(mesh):
     return jax.shard_map(
-        local,
+        block,
         mesh=mesh,
         in_specs=(
             P("dp", "space", None, None, None),

time: 423 us -> 48.2 us (0.11)
  waiting for transfers between devices: 243 us -> 0 us
  blocking collectives: 101 us -> 0 us
  Pallas kernels: 0 us -> 43.6 us
  local copies, waits for them, and re-layouts: 29.2 us -> 3.73 us
  starting transfers between devices: 14.3 us -> 0 us
  between operations: 14.7 us -> 0.66 us
  matrix products: 11.2 us -> 0 us
  other arithmetic: 8.8 us -> 0 us
    unnamed x5 -> x0, waiting for transfers between devices: 227 us -> none
    all_gather x2 -> x0, blocking collectives: 89 us -> none  [apply_weight(): whole = lax.all_gather(shard, 'dp', axis=0, tiled=True)]
    pallas_call x0 -> x1, Pallas kernels: none -> 43.6 us  [fused(): pl.pallas_call(functools.partial(block_kernel, sizes), out_shape=(jax.Sha...]
    psum x1 -> x0, waiting for transfers between devices: 16.8 us -> none  [reduce_grad(): return lax.psum(own_rows, 'space')]
    unnamed x129 -> x10, local copies, waits for them, and re-layouts: 19.9 us -> 3.73 us
    ppermute x8 -> x0, starting transfers between devices: 14.2 us -> none  [the longest x4 8.9 us: with_halo(): lax.ppermute(tail, axis, [(i, (i + 1) % count) for i in range(ends)])]
    psum x4 -> x0, blocking collectives: 12 us -> none  [the longest x2 6.27 us: normalize(): lax.psum((jnp.sum(values, axis=0), jnp.sum(values * values, axis=0)), 'sp...]
    dot_general x6 -> x0, matrix products: 11.2 us -> none  [the longest x2 5.29 us: reduce_grad(): lax.dot_general(unfolded, delta, (((0,), (0,)), ((), ())), preferred_elem...]
  transfers between devices with their start and end apart: 11 -> 0, of which waited for: 3 -> 0; matrix products, arithmetic and copies ran while one was open for 8% -> 0% of each run, Pallas kernels for 0% -> 0%
where the time goes in v1:
time: 48.2 us; the launch traced here: 48 us
  Pallas kernels  43.6 us (90%)
  local copies, waits for them, and re-layouts  3.73 us (8%)
  between operations  0.66 us (1%)
    pallas_call x1, Pallas kernels, fused(): pl.pallas_call(functools.partial(block_kernel, sizes), out_shape=(jax.Sha...  43.6 us
    unnamed x10, local copies, waits for them, and re-layouts  3.73 us

profile of v1, /device:TPU:0, one launch (start us, length us, event | category | flops | bytes accessed | tf_op | source)
XLA Modules:
  0.0 48.0 jit_solution(12346551173659350883)
XLA Ops:
  0.6 43.6 %shard_map.75 = (bf16[256,128]{1,0:T(8,128)(2,1)}, bf16[256,128]{1,0:T(8,128)(2,1)}, f32[216,128]{1,0:T(8,128)}, f32[216,128]{1,0:T(8,128)}) custom-call(bf16[256,128]{1,0:T(8,128)(2,1)} %bitcast.6, bf16[256,128]{1,0:T(8,128)(2,1)} %bitcast.7, bf16[216,128]{1,0:T(8,128)(2,1)} %first_ref.1, bf16[216,128]{1,0:T(8,128)(2,1)} %second_ref.1), custom_call_target="tpu_custom_call" | custom-call | flops 2717908992 | bytes 393216 | tf_op jit(solution)/shard_map/pallas_call | solution.py:492
  44.2 0.0 copy-start.2
  44.2 0.0 copy-start.1
  44.2 1.5 %copy.12 = bf16[1,4,8,8,128]{4,3,2,1,0:T(8,128)(2,1)} copy(bf16[1,4,8,8,128]{4,3,2,1,0:T(8,128)(2,1)} %bitcast.5) | data formatting | bytes 131072
  45.7 0.0 copy-done.2
  45.7 0.6 %copy.13 = bf16[1,4,8,8,128]{4,3,2,1,0:T(8,128)(2,1)} copy(bf16[1,4,8,8,128]{4,3,2,1,0:T(8,128)(2,1)S(1)} %bitcast.4) | data formatting | bytes 131072
  46.4 0.0 copy-done.1
  46.4 0.0 copy-start
  46.4 0.6 %copy.14 = f32[216,128]{1,0:T(8,128)} copy(f32[216,128]{1,0:T(8,128)S(1)} %copy-done.1) | data formatting | bytes 221184
  47.0 0.3 copy-done
  47.3 0.6 %copy.15 = f32[216,128]{1,0:T(8,128)} copy(f32[216,128]{1,0:T(8,128)S(1)} %copy-done) | data formatting | bytes 221184
Async XLA Ops:
  44.2 1.5 %copy-start.2 = (bf16[256,128]{1,0:T(8,128)(2,1)S(1)}, bf16[256,128]{1,0:T(8,128)(2,1)}, u32[]{:S(2)}) copy-start(bf16[256,128]{1,0:T(8,128)(2,1)} %get-tuple-element.9) | copy-start | bytes 196612
  44.2 2.2 %copy-start.1 = (f32[216,128]{1,0:T(8,128)S(1)}, f32[216,128]{1,0:T(8,128)}, u32[]{:S(2)}) copy-start(f32[216,128]{1,0:T(8,128)} %get-tuple-element.18) | copy-start | bytes 331780
  46.4 0.9 %copy-start = (f32[216,128]{1,0:T(8,128)S(1)}, f32[216,128]{1,0:T(8,128)}, u32[]{:S(2)}) copy-start(f32[216,128]{1,0:T(8,128)} %get-tuple-element.19) | copy-start | bytes 331780

commit v2 on v1

--- a/solution.py
+++ b/solution.py
@@ -215,12 +215,26 @@
     p = lax.rem(me, inner)
     sibling = (me, 1 - core)
 
+    def flipped(value, mask):
+        bit = 1
+        while bit <= mask:
+            if mask & bit:
+                value = value + bit - 2 * bit * lax.rem(lax.div(value, bit), 2)
+            bit *= 2
+        return value
+
     def line_peer(s):
-        return lax.rem(z + s, outer), lax.rem(z - s + outer, outer)
+        return flipped(z, s)
 
     def plane_peer(s):
-        return lax.rem(p + s, inner), lax.rem(p - s + inner, inner)
-
+        return flipped(p, s)
+
+    barrier = pltpu.get_barrier_semaphore()
+    partners = [sibling]
+    partners += [(line_peer(s) * inner + p, core) for s in range(1, outer)]
+    partners += [(z * inner + plane_peer(s), core) for s in range(1, inner)]
+    for device in partners:
+        pl.semaphore_signal(barrier, inc=1, device_id=device, device_id_type=MESH)
     for w, ref in enumerate((first_ref, second_ref)):
         own = jnp.concatenate(
             [
@@ -232,12 +246,6 @@
         mine = jnp.where(core == 0, own[:half], own[half:])
         gathered[w, core, me] = mine.astype(jnp.bfloat16)
 
-    barrier = pltpu.get_barrier_semaphore()
-    partners = [sibling]
-    partners += [(line_peer(s)[0] * inner + p, core) for s in range(1, outer)]
-    partners += [(z * inner + plane_peer(s)[0], core) for s in range(1, inner)]
-    for device in partners:
-        pl.semaphore_signal(barrier, inc=1, device_id=device, device_id_type=MESH)
     pl.semaphore_wait(barrier, len(partners))
 
     sends = []
@@ -255,26 +263,25 @@
         return remote(place, place, plane_ws.at[w, t, s], plane_wr.at[w, t, s], (target, core))
 
     def core_copy(w, t, which):
-        group = pl.ds(line_peer(t)[1] * inner, inner)
+        group = pl.ds(line_peer(t) * inner, inner)
         place = gathered.at[w, which, group]
         return remote(place, place, core_ws.at[w, t], core_wr.at[w, t], sibling)
 
     def send_line(w):
         for s in range(1, outer):
-            start(line_copy(w, s, me, line_peer(s)[0] * inner + p))
-
-    def send_plane(w):
-        for t in range(outer):
-            source = line_peer(t)[1] * inner + p
-            if t > 0:
-                line_copy(w, t, source, me).wait_recv()
-            for s in range(1, inner):
-                start(plane_copy(w, t, s, source, z * inner + plane_peer(s)[0]))
+            start(line_copy(w, s, me, line_peer(s) * inner + p))
+
+    def send_plane(w, t):
+        source = line_peer(t) * inner + p
+        if t > 0:
+            line_copy(w, t, source, me).wait_recv()
+        for s in range(1, inner):
+            start(plane_copy(w, t, s, source, z * inner + plane_peer(s)))
 
     def send_core(w):
         for t in range(outer):
             for s in range(1, inner):
-                source = line_peer(t)[1] * inner + plane_peer(s)[1]
+                source = line_peer(t) * inner + plane_peer(s)
                 plane_copy(w, t, s, source, me).wait_recv()
             start(core_copy(w, t, core))
 
@@ -365,22 +372,23 @@
                 grad_rows[g, k * channels : (k + 1) * channels, :] = result[
                     rest * channels : (rest + 1) * channels, a * channels : (a + 1) * channels
                 ]
-        for s in range(1, inner):
-            target = plane_peer(s)[0]
-            for t in range(outer):
-                grad_send[g, s, t] = own_part(g, t * inner + target).astype(jnp.bfloat16)
-            start(plane_grad_copy(g, s, z * inner + target))
+        for t in reversed(range(outer)):
+            for s in range(1, inner):
+                target = plane_peer(s)
+                part = own_part(g, line_peer(t) * inner + target)
+                grad_send[g, s, t] = part.astype(jnp.bfloat16)
+                start(plane_grad_copy(g, s, t, z * inner + target))
 
     def own_part(g, d):
         offset = pl.multiple_of(d * rows + core * half, 8)
         return grad_rows[g, pl.ds(offset, half), :]
 
-    def plane_grad_copy(g, s, target):
+    def plane_grad_copy(g, s, t, target):
         return remote(
-            grad_send.at[g, s],
-            grad_recv.at[g, s],
-            plane_gs.at[g, s],
-            plane_gr.at[g, s],
+            grad_send.at[g, s, t],
+            grad_recv.at[g, s, t],
+            plane_gs.at[g, s, t],
+            plane_gr.at[g, s, t],
             (target, core),
         )
 
@@ -398,19 +406,17 @@
         return remote(place, place, core_gs.at[g], core_gr.at[g], sibling)
 
     def reduce_plane(g):
-        for s in range(1, inner):
-            plane_grad_copy(g, s, me).wait_recv()
-        for t in range(1, outer):
-            target = line_peer(t)[0]
-            total = own_part(g, target * inner + p)
+        for t in reversed(range(outer)):
+            target = line_peer(t) * inner + p
+            total = own_part(g, target)
             for s in range(1, inner):
-                total = total + grad_recv[g, s, target].astype(jnp.float32)
-            line_send[g, t] = total.astype(jnp.bfloat16)
-            start(line_grad_copy(g, t, target * inner + p))
-        total = own_part(g, me)
-        for s in range(1, inner):
-            total = total + grad_recv[g, s, z].astype(jnp.float32)
-        halves[g, core] = total
+                plane_grad_copy(g, s, t, me).wait_recv()
+                total = total + grad_recv[g, s, t].astype(jnp.float32)
+            if t > 0:
+                line_send[g, t] = total.astype(jnp.bfloat16)
+                start(line_grad_copy(g, t, target))
+            else:
+                halves[g, core] = total
 
     def reduce_line(g):
         total = halves[g, core]
@@ -426,6 +432,8 @@
         ref[half:rows, :] = halves[g, 1][: rows - half]
 
     send_line(0)
+    send_plane(0, 0)
+    send_plane(1, 0)
     own_rows = pl.ds(pl.multiple_of(core * own_cells, own_cells), own_cells)
     other_rows = pl.ds(pl.multiple_of((1 - core) * own_cells, own_cells), own_cells)
     for f, ref in enumerate((image_ref, cotangent_ref)):
@@ -433,16 +441,19 @@
             remote(ref, fields.at[f, own_rows], field_send.at[f], field_recv.at[f], sibling)
         )
         fields[f, own_rows, :] = ref[...]
+    send_plane(0, 1)
     send_line(1)
+    for t in range(2, outer):
+        send_plane(0, t)
     grad_rows[:, count * rows :, :] = jnp.zeros_like(grad_rows[:, count * rows :, :])
-    send_plane(0)
     for f, ref in enumerate((image_ref, cotangent_ref)):
         remote(
             ref, fields.at[f, other_rows], field_send.at[f], field_recv.at[f], sibling
         ).wait_recv()
     spread(image_cols, fields[0].astype(jnp.float32))
+    for t in range(1, outer):
+        send_plane(1, t)
     send_core(0)
-    send_plane(1)
     finish_weight(0)
 
     first_norm, first_inverse = normalize(forward(image_cols, 0))
@@ -463,18 +474,32 @@
     first_delta = norm_back(inner_grad * gelu_slope(first_norm), first_norm, first_inverse)
     first_delta = first_delta.astype(jnp.bfloat16).astype(jnp.float32)
     weight_grad(image_cols, first_delta, 0)
-    reduce_plane(1)
     spread(delta_cols, first_delta)
     outer_ref[...] = outer_ref[...] + backward(delta_cols, 0)
     image_grad_ref[...] = outer_ref[own_rows, :].astype(jnp.bfloat16)
     output_ref[...] = gelu_value(summed_ref[own_rows, :]).astype(jnp.bfloat16)
+    reduce_plane(1)
+    reduce_plane(0)
     reduce_line(1)
-    reduce_plane(0)
     write_grad(1, second_grad_ref)
     reduce_line(0)
     write_grad(0, first_grad_ref)
     for copy in sends:
         copy.wait_send()
+
+
+def hand_over(*results):
+    def kernel(*refs):
+        for source, target in zip(refs[: len(results)], refs[len(results) :]):
+            target[...] = source[...]
+
+    whole = pl.BlockSpec(memory_space=pltpu.VMEM)
+    return pl.pallas_call(
+        kernel,
+        out_shape=tuple(jax.ShapeDtypeStruct(x.shape, x.dtype) for x in results),
+        in_specs=[whole] * len(results),
+        out_specs=(whole,) * len(results),
+    )(*results)
 
 
 def fused(count, image, cotangent, first_weight, second_weight):
@@ -525,8 +550,8 @@
             dma((2, outer, inner)),
             dma((2, outer)),
             dma((2, outer)),
-            dma((2, inner)),
-            dma((2, inner)),
+            dma((2, inner, outer)),
+            dma((2, inner, outer)),
             dma((2, outer)),
             dma((2, outer)),
             dma((2,)),
@@ -546,6 +571,9 @@
         first_weight,
         second_weight,
     )
+    output, image_grad, first_grad, second_grad = hand_over(
+        output, image_grad, first_grad, second_grad
+    )
     return output.reshape(image.shape), image_grad.reshape(image.shape), first_grad, second_grad
 
 
@@ -558,6 +586,7 @@
         and image.shape[0] == 1
         and inner > 1
         and count // inner > 1
+        and (count & (count - 1)) == 0
         and width % 8 == 0
         and channels % 128 == 0
         and rows % 8 == 0

time: 48.2 us -> 42 us (0.87)
  local copies, waits for them, and re-layouts: 3.73 us -> 0 us
  Pallas kernels: 43.6 us -> 41.1 us
    pallas_call x1, Pallas kernels: 43.6 us -> 39.3 us  [fused(): pl.pallas_call(functools.partial(block_kernel, sizes), out_shape=(jax.Sha...]
    unnamed x10 -> x0, local copies, waits for them, and re-layouts: 3.73 us -> none
    pallas_call x0 -> x1, Pallas kernels: none -> 1.76 us  [hand_over(): pl.pallas_call(kernel, out_shape=tuple((jax.ShapeDtypeStruct(x.shape, x.d...]
where the time goes in v2:
time: 42 us; the launch traced here: 41.7 us
  Pallas kernels  41.1 us (98%)
  between operations  0.64 us (2%)
    pallas_call x1, Pallas kernels, fused(): pl.pallas_call(functools.partial(block_kernel, sizes), out_shape=(jax.Sha...  39.3 us
    pallas_call x1, Pallas kernels, hand_over(): pl.pallas_call(kernel, out_shape=tuple((jax.ShapeDtypeStruct(x.shape, x.d...  1.76 us

profile of v2, /device:TPU:0, one launch (start us, length us, event | category | flops | bytes accessed | tf_op | source)
XLA Modules:
  0.0 41.7 jit_solution(2915436219541190731)
XLA Ops:
  0.6 39.3 %shard_map.75 = (bf16[256,128]{1,0:T(8,128)(2,1)}, bf16[256,128]{1,0:T(8,128)(2,1)}, f32[216,128]{1,0:T(8,128)}, f32[216,128]{1,0:T(8,128)}) custom-call(bf16[256,128]{1,0:T(8,128)(2,1)} %bitcast.4, bf16[256,128]{1,0:T(8,128)(2,1)} %bitcast.5, bf16[216,128]{1,0:T(8,128)(2,1)} %first_ref.1, bf16[216,128]{1,0:T(8,128)(2,1)} %second_ref.1), custom_call_target="tpu_custom_call" | custom-call | flops 2717908992 | bytes 393216 | tf_op jit(solution)/shard_map/pallas_call | solution.py:517
  40.0 1.8 %shard_map.76 = (bf16[256,128]{1,0:T(8,128)(2,1)}, bf16[256,128]{1,0:T(8,128)(2,1)}, f32[216,128]{1,0:T(8,128)}, f32[216,128]{1,0:T(8,128)}) custom-call(bf16[256,128]{1,0:T(8,128)(2,1)} %get-tuple-element.12.refs_0_, bf16[256,128]{1,0:T(8,128)(2,1)} %get-tuple-element.13.refs_1_, f32[216,128]{1,0:T(8,128)} %get-tuple-element.14.refs_2_, ...), custom_call_target="tpu_custom_call" | custom-call | tf_op jit(solution)/shard_map/pallas_call | solution.py:497

commit v3 on v2

--- a/solution.py
+++ b/solution.py
@@ -182,6 +182,8 @@
     grad_rows,
     grad_send,
     grad_recv,
+    near_send,
+    near_recv,
     line_send,
     line_recv,
     halves,
@@ -197,6 +199,8 @@
     core_wr,
     plane_gs,
     plane_gr,
+    near_gs,
+    near_gr,
     line_gs,
     line_gr,
     core_gs,
@@ -278,8 +282,15 @@
         for s in range(1, inner):
             start(plane_copy(w, t, s, source, z * inner + plane_peer(s)))
 
+    def send_near(w):
+        for s in range(1, inner):
+            source = z * inner + plane_peer(s)
+            plane_copy(w, 0, s, source, me).wait_recv()
+            start(plane_copy(w, 1, s, source, line_peer(1) * inner + p))
+        start(core_copy(w, 0, core))
+
     def send_core(w):
-        for t in range(outer):
+        for t in range(1, outer):
             for s in range(1, inner):
                 source = line_peer(t) * inner + plane_peer(s)
                 plane_copy(w, t, s, source, me).wait_recv()
@@ -372,7 +383,11 @@
                 grad_rows[g, k * channels : (k + 1) * channels, :] = result[
                     rest * channels : (rest + 1) * channels, a * channels : (a + 1) * channels
                 ]
-        for t in reversed(range(outer)):
+        for s in reversed(range(inner)):
+            part = own_part(g, line_peer(1) * inner + plane_peer(s))
+            near_send[g, s] = part.astype(jnp.bfloat16)
+            start(near_grad_copy(g, s, line_peer(1) * inner + p))
+        for t in reversed(range(2, outer)):
             for s in range(1, inner):
                 target = plane_peer(s)
                 part = own_part(g, line_peer(t) * inner + target)
@@ -382,6 +397,15 @@
     def own_part(g, d):
         offset = pl.multiple_of(d * rows + core * half, 8)
         return grad_rows[g, pl.ds(offset, half), :]
+
+    def near_grad_copy(g, s, target):
+        return remote(
+            near_send.at[g, s],
+            near_recv.at[g, s],
+            near_gs.at[g, s],
+            near_gr.at[g, s],
+            (target, core),
+        )
 
     def plane_grad_copy(g, s, t, target):
         return remote(
@@ -405,22 +429,33 @@
         place = halves.at[g, which]
         return remote(place, place, core_gs.at[g], core_gr.at[g], sibling)
 
+    def reduce_near(g):
+        for s in reversed(range(inner)):
+            near_grad_copy(g, s, me).wait_recv()
+            target = z * inner + plane_peer(s)
+            total = own_part(g, target) + near_recv[g, s].astype(jnp.float32)
+            if s > 0:
+                grad_send[g, s, 0] = total.astype(jnp.bfloat16)
+                start(plane_grad_copy(g, s, 0, target))
+            else:
+                halves[g, core] = total
+
     def reduce_plane(g):
-        for t in reversed(range(outer)):
+        for t in reversed(range(2, outer)):
             target = line_peer(t) * inner + p
             total = own_part(g, target)
             for s in range(1, inner):
                 plane_grad_copy(g, s, t, me).wait_recv()
                 total = total + grad_recv[g, s, t].astype(jnp.float32)
-            if t > 0:
-                line_send[g, t] = total.astype(jnp.bfloat16)
-                start(line_grad_copy(g, t, target))
-            else:
-                halves[g, core] = total
+            line_send[g, t] = total.astype(jnp.bfloat16)
+            start(line_grad_copy(g, t, target))
 
     def reduce_line(g):
         total = halves[g, core]
-        for t in range(1, outer):
+        for s in range(1, inner):
+            plane_grad_copy(g, s, 0, me).wait_recv()
+            total = total + grad_recv[g, s, 0].astype(jnp.float32)
+        for t in range(2, outer):
             line_grad_copy(g, t, me).wait_recv()
             total = total + line_recv[g, t].astype(jnp.float32)
         halves[g, core] = total * factor
@@ -432,6 +467,7 @@
         ref[half:rows, :] = halves[g, 1][: rows - half]
 
     send_line(0)
+    send_line(1)
     send_plane(0, 0)
     send_plane(1, 0)
     own_rows = pl.ds(pl.multiple_of(core * own_cells, own_cells), own_cells)
@@ -441,8 +477,8 @@
             remote(ref, fields.at[f, own_rows], field_send.at[f], field_recv.at[f], sibling)
         )
         fields[f, own_rows, :] = ref[...]
-    send_plane(0, 1)
-    send_line(1)
+    line_copy(0, 1, line_peer(1) * inner + p, me).wait_recv()
+    send_near(0)
     for t in range(2, outer):
         send_plane(0, t)
     grad_rows[:, count * rows :, :] = jnp.zeros_like(grad_rows[:, count * rows :, :])
@@ -451,7 +487,9 @@
             ref, fields.at[f, other_rows], field_send.at[f], field_recv.at[f], sibling
         ).wait_recv()
     spread(image_cols, fields[0].astype(jnp.float32))
-    for t in range(1, outer):
+    send_near(1)
+    line_copy(1, 1, line_peer(1) * inner + p, me).wait_recv()
+    for t in range(2, outer):
         send_plane(1, t)
     send_core(0)
     finish_weight(0)
@@ -479,7 +517,9 @@
     image_grad_ref[...] = outer_ref[own_rows, :].astype(jnp.bfloat16)
     output_ref[...] = gelu_value(summed_ref[own_rows, :]).astype(jnp.bfloat16)
     reduce_plane(1)
+    reduce_near(1)
     reduce_plane(0)
+    reduce_near(0)
     reduce_line(1)
     write_grad(1, second_grad_ref)
     reduce_line(0)
@@ -537,6 +577,8 @@
             pltpu.VMEM((2, 27 * channels + 2 * half - rows, channels), f32),
             pltpu.VMEM((2, inner, outer, half, channels), bf16),
             pltpu.VMEM((2, inner, outer, half, channels), bf16),
+            pltpu.VMEM((2, inner, half, channels), bf16),
+            pltpu.VMEM((2, inner, half, channels), bf16),
             pltpu.VMEM((2, outer, half, channels), bf16),
             pltpu.VMEM((2, outer, half, channels), bf16),
             pltpu.VMEM((2, 2, half, channels), f32),
@@ -552,6 +594,8 @@
             dma((2, outer)),
             dma((2, inner, outer)),
             dma((2, inner, outer)),
+            dma((2, inner)),
+            dma((2, inner)),
             dma((2, outer)),
             dma((2, outer)),
             dma((2,)),

time: 42 us -> 38.1 us (0.907)
  Pallas kernels: 41.1 us -> 37.2 us
    pallas_call x1, Pallas kernels: 39.3 us -> 35.5 us  [fused(): pl.pallas_call(functools.partial(block_kernel, sizes), out_shape=(jax.Sha...]
where the time goes in v3:
time: 38.1 us; the launch traced here: 37.9 us
  Pallas kernels  37.2 us (98%)
  between operations  0.64 us (2%)
    pallas_call x1, Pallas kernels, fused(): pl.pallas_call(functools.partial(block_kernel, sizes), out_shape=(jax.Sha...  35.5 us
    pallas_call x1, Pallas kernels, hand_over(): pl.pallas_call(kernel, out_shape=tuple((jax.ShapeDtypeStruct(x.shape, x.d...  1.76 us

profile of v3, /device:TPU:0, one launch (start us, length us, event | category | flops | bytes accessed | tf_op | source)
XLA Modules:
  0.0 37.9 jit_solution(11388730815917466113)
XLA Ops:
  0.6 35.5 %shard_map.75 = (bf16[256,128]{1,0:T(8,128)(2,1)}, bf16[256,128]{1,0:T(8,128)(2,1)}, f32[216,128]{1,0:T(8,128)}, f32[216,128]{1,0:T(8,128)}) custom-call(bf16[256,128]{1,0:T(8,128)(2,1)} %bitcast.4, bf16[256,128]{1,0:T(8,128)(2,1)} %bitcast.5, bf16[216,128]{1,0:T(8,128)(2,1)} %first_ref.1, bf16[216,128]{1,0:T(8,128)(2,1)} %second_ref.1), custom_call_target="tpu_custom_call" | custom-call | flops 2717908992 | bytes 393216 | tf_op jit(solution)/shard_map/pallas_call | solution.py:557
  36.1 1.8 %shard_map.76 = (bf16[256,128]{1,0:T(8,128)(2,1)}, bf16[256,128]{1,0:T(8,128)(2,1)}, f32[216,128]{1,0:T(8,128)}, f32[216,128]{1,0:T(8,128)}) custom-call(bf16[256,128]{1,0:T(8,128)(2,1)} %get-tuple-element.12.refs_0_, bf16[256,128]{1,0:T(8,128)(2,1)} %get-tuple-element.13.refs_1_, f32[216,128]{1,0:T(8,128)} %get-tuple-element.14.refs_2_, ...), custom_call_target="tpu_custom_call" | custom-call | tf_op jit(solution)/shard_map/pallas_call | solution.py:537
